TPU v7x, 512 devices: a whole 4x8x8 slice. The times are simulated.
512 devices in a mesh: slab: 128 (over z_lo, x, y, core), pencil: 4 (over z_hi).
Axes of the slice: x: 4, y: 8, z: 8 (z_hi: 4, z_lo: 2; z = z_hi * 2 + z_lo), core: 2. Of those that a mesh axis runs over, the one named last changes fastest.
Arguments:
- density: float32 [256, 256, 256], P('slab', 'pencil'), may hold values from -6 to 6
- weight_down: bfloat16 [48, 24], replicated, may hold values from -1.25 to 1.25
- bias_down: float32 [48], replicated, may hold values from -3 to 3
- weight_conv: bfloat16 [27, 48, 48], replicated, may hold values from -0.15625 to 0.15625
- bias_conv: float32 [48], replicated, may hold values from -3 to 3
- weight_out: bfloat16 [3, 48], replicated, may hold values from -0.875 to 0.875
- observed: float32 [3, 128, 128, 128], P(None, 'slab', 'pencil'), may hold values from -6 to 6
- noise_precision: float32 [128, 128, 128], P('slab', 'pencil'), may hold values from 0.25 to 4
Outputs:
- gradient: float32 [256, 256, 256], P('slab', 'pencil')
All inputs are finite; a program needn't handle non-finite values.
Results may differ from a plain program's by a relative error of at most 0.0033.
Values may be sent and summed in bfloat16 or wider, within the bound.
A program may use at most 128 MiB of HBM per device.

v0:
```python
import math

import jax
import jax.numpy as jnp
from jax import lax
from jax.sharding import PartitionSpec as P

growth_factor = 3.0
highest = lax.Precision.HIGHEST


def with_halo(block, sides, width):
    for axis, dim in sides:
        count = lax.axis_size(axis)
        forward = [(i, i + 1) for i in range(count - 1)]
        forward.append((count - 1, 0))
        backward = [(target, source) for source, target in forward]
        low = lax.ppermute(
            lax.slice_in_dim(block, block.shape[dim] - width, None, axis=dim), axis, forward
        )
        high = lax.ppermute(lax.slice_in_dim(block, 0, width, axis=dim), axis, backward)
        block = jnp.concatenate([low, block, high], axis=dim)
    return block


def fourier_table(length):
    indices = jnp.arange(length, dtype=jnp.int32)
    phases = indices[:, None] * indices[None, :] % length
    angles = phases.astype(jnp.float32) * (2.0 * math.pi / length)
    return (jnp.cos(angles), jnp.sin(angles))


def half_table(length, weights):
    half_count = length // 2
    positions = jnp.arange(length, dtype=jnp.int32)
    numbers = jnp.arange(half_count, dtype=jnp.int32)
    phases = positions[:, None] * numbers[None, :] % length
    angles = phases.astype(jnp.float32) * (2.0 * math.pi / length)
    return (jnp.cos(angles) * weights[None, :], jnp.sin(angles) * weights[None, :])


def wave_axis(length, count, offset):
    indices = offset + jnp.arange(count, dtype=jnp.int32)
    signed = jnp.where(indices < length // 2, indices, indices - length)
    numerator = jnp.where(indices == length // 2, 0, signed)
    spacing = 2.0 * math.pi / length
    return (indices, numerator.astype(jnp.float32) * spacing, signed.astype(jnp.float32) * spacing)


def multipliers(grid_x, grid_y, grid_z, count_y, count_z, start_y, start_z):
    index_x, along_x, full_x = wave_axis(grid_x, grid_x, 0)
    index_y, along_y, full_y = wave_axis(grid_y, count_y, start_y)
    index_z, along_z, full_z = wave_axis(grid_z, count_z, start_z)
    square = (
        (full_y * full_y)[:, None, None]
        + (full_z * full_z)[None, :, None]
        + (full_x * full_x)[None, None, :]
    )
    anchor = (
        (index_y[:, None, None] == 0)
        & (index_z[None, :, None] == 0)
        & (index_x[None, None, :] == 0)
    )
    square = square + anchor.astype(jnp.float32)
    extent = square.shape
    numerators = jnp.stack(
        [
            jnp.broadcast_to(along_x[None, None, :], extent),
            jnp.broadcast_to(along_y[:, None, None], extent),
            jnp.broadcast_to(along_z[None, :, None], extent),
        ]
    )
    return growth_factor * numerators / square[None]


def complex_mix(cosine_part, sine_part, sign):
    if sign < 0:
        return jnp.stack(
            [cosine_part[:, 0] + sine_part[:, 1], cosine_part[:, 1] - sine_part[:, 0]], axis=1
        )
    return jnp.stack(
        [cosine_part[:, 0] - sine_part[:, 1], cosine_part[:, 1] + sine_part[:, 0]], axis=1
    )


def forward_transform(values, z_pair, y_pair, x_pair):
    real_part = jnp.einsum("mxyz,zk->mxky", values, z_pair[0], precision=highest)
    imag_part = -jnp.einsum("mxyz,zk->mxky", values, z_pair[1], precision=highest)
    spectrum = jnp.stack([real_part, imag_part], axis=1)
    section = lax.all_to_all(spectrum, "pencil", split_axis=3, concat_axis=4, tiled=True)
    cosine_part = jnp.einsum("mcxky,yq->mcxqk", section, y_pair[0], precision=highest)
    sine_part = jnp.einsum("mcxky,yq->mcxqk", section, y_pair[1], precision=highest)
    mixed = complex_mix(cosine_part, sine_part, -1)
    section = lax.all_to_all(mixed, "slab", split_axis=3, concat_axis=2, tiled=True)
    cosine_part = jnp.einsum("mcxqk,xp->mcqkp", section, x_pair[0], precision=highest)
    sine_part = jnp.einsum("mcxqk,xp->mcqkp", section, x_pair[1], precision=highest)
    return complex_mix(cosine_part, sine_part, -1)


def inverse_transform(spectrum, z_pair, y_pair, x_pair):
    cosine_part = jnp.einsum("mcqkp,px->mcxqk", spectrum, x_pair[0], precision=highest)
    sine_part = jnp.einsum("mcqkp,px->mcxqk", spectrum, x_pair[1], precision=highest)
    summed = complex_mix(cosine_part, sine_part, 1)
    section = lax.all_to_all(summed, "slab", split_axis=2, concat_axis=3, tiled=True)
    cos_rows = jnp.einsum("mcxqk,qy->mcxky", section, y_pair[0], precision=highest)
    sin_rows = jnp.einsum("mcxqk,qy->mcxky", section, y_pair[1], precision=highest)
    mixed = complex_mix(cos_rows, sin_rows, 1)
    section = lax.all_to_all(mixed, "pencil", split_axis=4, concat_axis=3, tiled=True)
    return jnp.einsum("mxky,zk->mxyz", section[:, 0], z_pair[0], precision=highest) - jnp.einsum(
        "mxky,zk->mxyz", section[:, 1], z_pair[1], precision=highest
    )


def extend_margins(values, width):
    return with_halo(values, (("slab", 1), ("pencil", 2)), width)


def gate_slope(values):
    sigmoid = jax.nn.sigmoid(values)
    return sigmoid * (1.0 + values * (1.0 - sigmoid))


def down_sample(values, kernel, offsets):
    channels_in, extent_x, extent_y, extent_z = values.shape
    grouped = values.reshape(channels_in, extent_x // 2, 2, extent_y // 2, 2, extent_z // 2, 2)
    summed = jnp.einsum("oiabc,ixaybzc->oxyz", kernel, grouped, preferred_element_type=jnp.float32)
    return summed + offsets[:, None, None, None]


def stencil(framed, weights):
    extent_x = framed.shape[1] - 2
    extent_y = framed.shape[2] - 2
    extent_z = framed.shape[3]
    wrapped = jnp.concatenate([framed[..., -1:], framed, framed[..., :1]], axis=3)
    summed = None
    for shift_x in range(3):
        for shift_y in range(3):
            stacked = jnp.stack(
                [
                    wrapped[
                        :,
                        shift_x : shift_x + extent_x,
                        shift_y : shift_y + extent_y,
                        shift_z : shift_z + extent_z,
                    ]
                    for shift_z in range(3)
                ]
            )
            first_tap = shift_x * 9 + shift_y * 3
            partial_sum = jnp.einsum(
                "toc,tcxyz->oxyz",
                weights[first_tap : first_tap + 3],
                stacked,
                preferred_element_type=jnp.float32,
            )
            summed = partial_sum if summed is None else summed + partial_sum
    return summed


def on_device(
    density, weight_down, bias_down, weight_conv, bias_conv, weight_out, observed, noise_precision
):
    planes, local_y, grid_z = density.shape
    grid_x = planes * lax.axis_size("slab")
    grid_y = local_y * lax.axis_size("pencil")
    half_z = grid_z // 2
    count_y = grid_y // lax.axis_size("slab")
    count_z = half_z // lax.axis_size("pencil")
    channels = weight_down.shape[0]
    cells_total = float(grid_x * grid_y * grid_z)
    plain_weights = jnp.ones((half_z,), jnp.float32)
    doubled = (
        jnp.where(jnp.arange(half_z, dtype=jnp.int32) == 0, 1.0, 2.0).astype(jnp.float32)
        / cells_total
    )
    z_plain = half_table(grid_z, plain_weights)
    z_scaled = half_table(grid_z, doubled)
    y_pair = fourier_table(grid_y)
    x_pair = fourier_table(grid_x)
    factors = multipliers(
        grid_x,
        grid_y,
        grid_z,
        count_y,
        count_z,
        lax.axis_index("slab") * count_y,
        lax.axis_index("pencil") * count_z,
    )
    spectrum = forward_transform(density[None], z_plain, y_pair, x_pair)[0]
    displaced_hat = jnp.stack([-factors * spectrum[1], factors * spectrum[0]], axis=1)
    displaced = inverse_transform(displaced_hat, z_scaled, y_pair, x_pair).astype(jnp.bfloat16)
    kernel_down = weight_down.reshape(channels, 3, 2, 2, 2)
    pre_down = down_sample(displaced, kernel_down, bias_down)
    framed = extend_margins(jax.nn.silu(pre_down).astype(jnp.bfloat16), 1)
    pre_conv = stencil(framed, weight_conv) + bias_conv[:, None, None, None]
    hidden = jax.nn.silu(pre_conv).astype(jnp.bfloat16)
    predicted = jnp.einsum("jo,oxyz->jxyz", weight_out, hidden, preferred_element_type=jnp.float32)
    residual = noise_precision[None] * (predicted - observed)
    grad_hidden = jnp.einsum(
        "jo,jxyz->oxyz", weight_out.astype(jnp.float32), residual, precision=highest
    )
    grad_conv = (grad_hidden * gate_slope(pre_conv)).astype(jnp.bfloat16)
    flipped = jnp.swapaxes(weight_conv[::-1], 1, 2)
    grad_down_in = stencil(extend_margins(grad_conv, 1), flipped)
    grad_down = (grad_down_in * gate_slope(pre_down)).astype(jnp.bfloat16)
    grad_fine = jnp.einsum(
        "oiabc,oxyz->ixaybzc", kernel_down, grad_down, preferred_element_type=jnp.float32
    ).reshape(3, planes, local_y, grid_z)
    grad_hat = forward_transform(grad_fine, z_scaled, y_pair, x_pair)
    combined = jnp.stack(
        [jnp.sum(factors * grad_hat[:, 1], axis=0), -jnp.sum(factors * grad_hat[:, 0], axis=0)]
    )
    return inverse_transform(combined[None], z_plain, y_pair, x_pair)[0]


def solution(mesh):
    return jax.shard_map(
        on_device,
        mesh=mesh,
        in_specs=(
            P("slab", "pencil", None),
            P(),
            P(),
            P(),
            P(),
            P(),
            P(None, "slab", "pencil", None),
            P("slab", "pencil", None),
        ),
        out_specs=P("slab", "pencil", None),
        check_vma=False,
    )
```

profile of v0, /device:TPU:1, one launch (start us, length us, event | category | flops | bytes accessed | tf_op | source)
XLA Modules:
  0.0 377.9 jit_solution(4210275541608767990)
XLA Ops:
  3.6 10.8 %all-to-all-start = ((f32[4,1,8192]{2,1,0:T(1,128)}), f32[4,1,8192]{2,1,0:T(1,128)S(1)}, u32[]{:S(2)}, u32[]{:S(2)}) async-start(f32[4,1,8192]{2,1,0:T(1,128)} %reshape.507), calls=%async_computation | async-start | bytes 262144 | tf_op jit(solution)/shard_map/all_to_all | solution.py:90
  14.7 7.3 %all-to-all-done = f32[4,1,8192]{2,1,0:T(1,128)S(1)} async-done(((f32[4,1,8192]{2,1,0:T(1,128)}), f32[4,1,8192]{2,1,0:T(1,128)S(1)}, u32[]{:S(2)}, u32[]{:S(2)}) %all-to-all-start) | async-done | bytes 131104 | tf_op jit(solution)/shard_map/all_to_all | solution.py:90
  28.3 13.9 %all-to-all-start.1 = ((f32[128,1,256]{2,1,0:T(1,128)}), f32[128,1,256]{2,1,0:T(1,128)S(1)}, u32[]{:S(2)}, u32[]{:S(2)}) async-start(f32[128,1,256]{2,1,0:T(1,128)} %reshape.509), calls=%async_computation.1 | async-start | bytes 262144 | tf_op jit(solution)/shard_map/all_to_all | solution.py:94
  42.3 11.5 %all-to-all-done.1 = f32[128,1,256]{2,1,0:T(1,128)S(1)} async-done(((f32[128,1,256]{2,1,0:T(1,128)}), f32[128,1,256]{2,1,0:T(1,128)S(1)}, u32[]{:S(2)}, u32[]{:S(2)}) %all-to-all-start.1) | async-done | bytes 131104 | tf_op jit(solution)/shard_map/all_to_all | solution.py:94
  64.8 21.2 %all_to_all.135 = f32[128,1,768]{2,1,0:T(1,128)S(1)} all-to-all(f32[128,1,768]{2,1,0:T(1,128)S(1)} %reshape.511), channel_id=1, replica_groups=mesh['slab'=128,'pencil'=4] {'slab'}, dimensions={0} | all-to-all | bytes 786432 | tf_op jit(solution)/shard_map/all_to_all | solution.py:104
  90.2 3.4 fusion.125
  93.7 3.4 fusion.139
  100.5 3.6 all-to-all-start.3
  104.2 12.1 %all-to-all-done.3 = f32[4,1,24576]{2,1,0:T(1,128)S(1)} async-done(((f32[4,1,24576]{2,1,0:T(1,128)}), f32[4,1,24576]{2,1,0:T(1,128)S(1)}, u32[]{:S(2)}, u32[]{:S(2)}) %all-to-all-start.3) | async-done | bytes 393248 | tf_op jit(solution)/shard_map/all_to_all | solution.py:108
  122.7 28.1 %reshape.433 = bf16[3,2,32,2,128,2]{5,4,3,2,1,0:T(8,128)(2,1)} reshape(bf16[3,2,64,256]{3,2,1,0:T(8,128)(2,1)S(1)} %fusion.107) | data formatting | bytes 393216 | tf_op jit(solution)/shard_map/reshape.33
  150.8 8.0 %multiply_convert_fusion.1 = (bf16[48,32,128]{2,0,1:T(8,128)(2,1)S(1)}, f32[48,32,128]{2,0,1:T(8,128)}) fusion(f32[48]{0:T(128)S(1)} %copy-done.8, bf16[48,3,2,2,2,1]{0,4,3,2,1,5:T(2,128)(2,1)S(1)} %bitcast.692, bf16[3,2,32,2,128,2]{5,4,3,2,1,0:T(8,128)(2,1)} %reshape.433), kind=kOutput, calls=%fused_computation.172 | convolution fusion | flops 10616832 | bytes 1378752 | tf_op jit(solution)/shard_map/oiabc,ixaybzc->oxyz/dot_general | solution.py:126
  158.8 4.4 %collective-permute-start = (bf16[48,1,32,128]{3,0,2,1:T(8,128)(2,1)S(1)}, bf16[48,1,32,128]{3,0,2,1:T(8,128)(2,1)S(1)}, u32[]{:S(2)}, u32[]{:S(2)}) collective-permute-start(bf16[48,1,32,128]{3,0,2,1:T(8,128)(2,1)S(1)} %bitcast.649), channel_id=1, source_target_pairs={{0,4},{4,8},{8,12},{12,16},{16,20},{20,24},{24,28},{28,32},{32,36}... | collective-permute-start | bytes 1179656 | tf_op jit(solution)/shard_map/ppermute | solution.py:18
  165.1 2.8 collective-permute-done
  167.8 4.7 %collective-permute-done.1 = bf16[48,1,32,128]{3,0,2,1:T(8,128)(2,1)S(1)} collective-permute-done((bf16[48,1,32,128]{3,0,2,1:T(8,128)(2,1)S(1)}, bf16[48,1,32,128]{3,0,2,1:T(8,128)(2,1)S(1)}, u32[]{:S(2)}, u32[]{:S(2)}) %collective-permute-start.1) | collective-permute-done | bytes 393248 | tf_op jit(solution)/shard_map/ppermute | solution.py:21
  172.6 4.7 %collective-permute-start.2 = (bf16[48,3,1,128]{3,0,2,1:T(8,128)(2,1)S(1)}, bf16[48,3,1,128]{3,0,2,1:T(8,128)(2,1)S(1)}, u32[]{:S(2)}, u32[]{:S(2)}) collective-permute-start(bf16[48,3,1,128]{3,0,2,1:T(8,128)(2,1)S(1)} %get-tuple-element.65), channel_id=1, source_target_pairs={{0,1},{1,2},{2,3},{3,0},{4,5},{5,6},{6,7},{7,4},{8,9},{9,10},{10,1... | collective-permute-start | bytes 110600 | tf_op jit(solution)/shard_map/ppermute | solution.py:18
  177.2 2.7 collective-permute-start.3
  180.0 3.4 collective-permute-done.3
  184.0 3.5 maximum_maximum_fusion
  194.3 3.4 collective-permute-start.4
  197.8 4.1 %collective-permute-start.5 = (bf16[48,1,32,128]{3,0,2,1:T(8,128)(2,1)S(1)}, bf16[48,1,32,128]{3,0,2,1:T(8,128)(2,1)S(1)}, u32[]{:S(2)}, u32[]{:S(2)}) collective-permute-start(bf16[48,1,32,128]{3,0,2,1:T(8,128)(2,1)S(1)} %bitcast.641), channel_id=1, source_target_pairs={{4,0},{8,4},{12,8},{16,12},{20,16},{24,20},{28,24},{32,28},{36,32}... | collective-permute-start | bytes 1179656 | tf_op jit(solution)/shard_map/ppermute | solution.py:21
  202.5 4.7 %collective-permute-done.5 = bf16[48,1,32,128]{3,0,2,1:T(8,128)(2,1)S(1)} collective-permute-done((bf16[48,1,32,128]{3,0,2,1:T(8,128)(2,1)S(1)}, bf16[48,1,32,128]{3,0,2,1:T(8,128)(2,1)S(1)}, u32[]{:S(2)}, u32[]{:S(2)}) %collective-permute-start.5) | collective-permute-done | bytes 393248 | tf_op jit(solution)/shard_map/ppermute | solution.py:21
  209.7 5.1 %collective-permute-start.7 = (bf16[48,3,1,128]{3,0,2,1:T(8,128)(2,1)S(1)}, bf16[48,3,1,128]{3,0,2,1:T(8,128)(2,1)S(1)}, u32[]{:S(2)}, u32[]{:S(2)}) collective-permute-start(bf16[48,3,1,128]{3,0,2,1:T(8,128)(2,1)S(1)} %get-tuple-element.64), channel_id=1, source_target_pairs={{1,0},{2,1},{3,2},{0,3},{5,4},{6,5},{7,6},{4,7},{9,8},{10,9},{11,1... | collective-permute-start | bytes 110600 | tf_op jit(solution)/shard_map/ppermute | solution.py:21
  216.3 3.4 maximum_maximum_fusion.1
  231.6 3.9 %convolution_bitcast_fusion.19 = f32[3,1,2,32,2,128,2]{5,0,6,4,2,3,1:T(4,128)S(1)} fusion(f32[32,128,48]{1,2,0:T(8,128)} %convolution_bitcast_fusion, f32[32,128,48]{1,2,0:T(8,128)} %convolution_bitcast_fusion.1, f32[32,128,48]{1,2,0:T(8,128)} %convolution_bitcast_fusion.2, f32[32,128,48]{1,2,0:T(8,128)} %convolution_bitcast_fusion.3, ...), kind=kOutput, calls=%fused_computation.53 | convolution fusion | flops 72941568 | bytes 8693760 | tf_op jit(solution)/shard_map/oiabc,oxyz->ixaybzc/dot_general | solution.py:206
  235.5 12.4 %copy.96 = f32[3,1,2,32,2,128,2]{6,5,4,3,2,0,1:T(8,128)} copy(f32[3,1,2,32,2,128,2]{5,0,6,4,2,3,1:T(4,128)S(1)} %convolution_bitcast_fusion.19) | data formatting | bytes 786432 | tf_op jit(solution)/shard_map/oiabc,oxyz->ixaybzc/transpose | solution.py:206
  247.9 18.4 %reshape.454 = f32[3,2,64,256]{3,2,1,0:T(8,128)S(1)} reshape(f32[3,1,2,32,2,128,2]{6,5,4,3,2,0,1:T(8,128)} %copy.96) | data formatting | bytes 786432 | tf_op jit(solution)/shard_map/reshape | solution.py:208
  269.8 14.8 %all_to_all.136 = f32[4,1,24576]{2,1,0:T(1,128)S(1)} all-to-all(f32[4,1,24576]{2,1,0:T(1,128)S(1)} %reshape.515), channel_id=1, replica_groups=mesh['slab'=128,'pencil'=4] {'pencil'}, dimensions={0} | all-to-all | bytes 786432 | tf_op jit(solution)/shard_map/all_to_all | solution.py:90
  293.6 31.0 %all_to_all.137 = f32[128,1,768]{2,1,0:T(1,128)S(1)} all-to-all(f32[128,1,768]{2,1,0:T(1,128)S(1)} %reshape.517), channel_id=1, replica_groups=mesh['slab'=128,'pencil'=4] {'slab'}, dimensions={0} | all-to-all | bytes 786432 | tf_op jit(solution)/shard_map/all_to_all | solution.py:94
  328.9 3.4 fusion.122
  332.3 3.4 fusion.136
  339.7 18.3 %all_to_all.138 = f32[128,1,256]{2,1,0:T(1,128)S(1)} all-to-all(f32[128,1,256]{2,1,0:T(1,128)S(1)} %reshape.519), channel_id=1, replica_groups=mesh['slab'=128,'pencil'=4] {'slab'}, dimensions={0} | all-to-all | bytes 262144 | tf_op jit(solution)/shard_map/all_to_all | solution.py:104
  364.0 9.7 %all_to_all.139 = f32[4,1,8192]{2,1,0:T(1,128)S(1)} all-to-all(f32[4,1,8192]{2,1,0:T(1,128)S(1)} %reshape.521), channel_id=1, replica_groups=mesh['slab'=128,'pencil'=4] {'pencil'}, dimensions={0} | all-to-all | bytes 262144 | tf_op jit(solution)/shard_map/all_to_all | solution.py:108
  (163 shorter events, 91.1 us)
Async XLA Ops:
  0.0 0.9 copy-start
  3.6 18.4 %all-to-all-start = ((f32[4,1,8192]{2,1,0:T(1,128)}), f32[4,1,8192]{2,1,0:T(1,128)S(1)}, u32[]{:S(2)}, u32[]{:S(2)}) async-start(f32[4,1,8192]{2,1,0:T(1,128)} %reshape.507), calls=%async_computation | async-start | bytes 262144 | tf_op jit(solution)/shard_map/all_to_all | solution.py:90
  28.3 25.5 %all-to-all-start.1 = ((f32[128,1,256]{2,1,0:T(1,128)}), f32[128,1,256]{2,1,0:T(1,128)S(1)}, u32[]{:S(2)}, u32[]{:S(2)}) async-start(f32[128,1,256]{2,1,0:T(1,128)} %reshape.509), calls=%async_computation.1 | async-start | bytes 262144 | tf_op jit(solution)/shard_map/all_to_all | solution.py:94
  100.5 15.8 %all-to-all-start.3 = ((f32[4,1,24576]{2,1,0:T(1,128)}), f32[4,1,24576]{2,1,0:T(1,128)S(1)}, u32[]{:S(2)}, u32[]{:S(2)}) async-start(f32[4,1,24576]{2,1,0:T(1,128)} %reshape.513), calls=%async_computation.3 | async-start | bytes 786432 | tf_op jit(solution)/shard_map/all_to_all | solution.py:108
  122.7 28.2 %copy-start.6 = (bf16[48,24]{0,1:T(8,128)(2,1)S(1)}, bf16[48,24]{0,1:T(8,128)(2,1)}, u32[]{:S(2)}) copy-start(bf16[48,24]{0,1:T(8,128)(2,1)} %param.9) | copy-start | bytes 6916
  122.7 28.1 %copy-start.8 = (f32[48]{0:T(128)S(1)}, f32[48]{0:T(128)}, u32[]{:S(2)}) copy-start(f32[48]{0:T(128)} %param.10) | copy-start | bytes 580
  158.8 9.1 %collective-permute-start = (bf16[48,1,32,128]{3,0,2,1:T(8,128)(2,1)S(1)}, bf16[48,1,32,128]{3,0,2,1:T(8,128)(2,1)S(1)}, u32[]{:S(2)}, u32[]{:S(2)}) collective-permute-start(bf16[48,1,32,128]{3,0,2,1:T(8,128)(2,1)S(1)} %bitcast.649), channel_id=1, source_target_pairs={{0,4},{4,8},{8,12},{12,16},{16,20},{20,24},{24,28},{28,32},{32,36}... | collective-permute-start | bytes 1179656 | tf_op jit(solution)/shard_map/ppermute | solution.py:18
  163.1 9.4 %collective-permute-start.1 = (bf16[48,1,32,128]{3,0,2,1:T(8,128)(2,1)S(1)}, bf16[48,1,32,128]{3,0,2,1:T(8,128)(2,1)S(1)}, u32[]{:S(2)}, u32[]{:S(2)}) collective-permute-start(bf16[48,1,32,128]{3,0,2,1:T(8,128)(2,1)S(1)} %bitcast.650), channel_id=1, source_target_pairs={{4,0},{8,4},{12,8},{16,12},{20,16},{24,20},{28,24},{32,28},{36,32}... | collective-permute-start | bytes 1179656 | tf_op jit(solution)/shard_map/ppermute | solution.py:21
  172.6 7.4 %collective-permute-start.2 = (bf16[48,3,1,128]{3,0,2,1:T(8,128)(2,1)S(1)}, bf16[48,3,1,128]{3,0,2,1:T(8,128)(2,1)S(1)}, u32[]{:S(2)}, u32[]{:S(2)}) collective-permute-start(bf16[48,3,1,128]{3,0,2,1:T(8,128)(2,1)S(1)} %get-tuple-element.65), channel_id=1, source_target_pairs={{0,1},{1,2},{2,3},{3,0},{4,5},{5,6},{6,7},{7,4},{8,9},{9,10},{10,1... | collective-permute-start | bytes 110600 | tf_op jit(solution)/shard_map/ppermute | solution.py:18
  177.2 6.1 %collective-permute-start.3 = (bf16[48,3,1,128]{3,0,2,1:T(8,128)(2,1)S(1)}, bf16[48,3,1,128]{3,0,2,1:T(8,128)(2,1)S(1)}, u32[]{:S(2)}, u32[]{:S(2)}) collective-permute-start(bf16[48,3,1,128]{3,0,2,1:T(8,128)(2,1)S(1)} %get-tuple-element.66), channel_id=1, source_target_pairs={{1,0},{2,1},{3,2},{0,3},{5,4},{6,5},{7,6},{4,7},{9,8},{10,9},{11,1... | collective-permute-start | bytes 110600 | tf_op jit(solution)/shard_map/ppermute | solution.py:21
  187.9 1.0 copy-start.2
  191.8 0.7 copy-start.3
  192.5 0.8 copy-start.4
  192.5 0.8 copy-start.5
  192.5 0.8 copy-start.7
  194.3 8.2 %collective-permute-start.4 = (bf16[48,1,32,128]{3,0,2,1:T(8,128)(2,1)S(1)}, bf16[48,1,32,128]{3,0,2,1:T(8,128)(2,1)S(1)}, u32[]{:S(2)}, u32[]{:S(2)}) collective-permute-start(bf16[48,1,32,128]{3,0,2,1:T(8,128)(2,1)S(1)} %bitcast.640), channel_id=1, source_target_pairs={{0,4},{4,8},{8,12},{12,16},{16,20},{20,24},{24,28},{28,32},{32,36}... | collective-permute-start | bytes 1179656 | tf_op jit(solution)/shard_map/ppermute | solution.py:18
  197.8 9.4 %collective-permute-start.5 = (bf16[48,1,32,128]{3,0,2,1:T(8,128)(2,1)S(1)}, bf16[48,1,32,128]{3,0,2,1:T(8,128)(2,1)S(1)}, u32[]{:S(2)}, u32[]{:S(2)}) collective-permute-start(bf16[48,1,32,128]{3,0,2,1:T(8,128)(2,1)S(1)} %bitcast.641), channel_id=1, source_target_pairs={{4,0},{8,4},{12,8},{16,12},{20,16},{24,20},{28,24},{32,28},{36,32}... | collective-permute-start | bytes 1179656 | tf_op jit(solution)/shard_map/ppermute | solution.py:21
  207.2 7.7 %collective-permute-start.6 = (bf16[48,3,1,128]{3,0,2,1:T(8,128)(2,1)S(1)}, bf16[48,3,1,128]{3,0,2,1:T(8,128)(2,1)S(1)}, u32[]{:S(2)}, u32[]{:S(2)}) collective-permute-start(bf16[48,3,1,128]{3,0,2,1:T(8,128)(2,1)S(1)} %get-tuple-element.63), channel_id=1, source_target_pairs={{0,1},{1,2},{2,3},{3,0},{4,5},{5,6},{6,7},{7,4},{8,9},{9,10},{10,1... | collective-permute-start | bytes 110600 | tf_op jit(solution)/shard_map/ppermute | solution.py:18
  209.7 6.0 %collective-permute-start.7 = (bf16[48,3,1,128]{3,0,2,1:T(8,128)(2,1)S(1)}, bf16[48,3,1,128]{3,0,2,1:T(8,128)(2,1)S(1)}, u32[]{:S(2)}, u32[]{:S(2)}) collective-permute-start(bf16[48,3,1,128]{3,0,2,1:T(8,128)(2,1)S(1)} %get-tuple-element.64), channel_id=1, source_target_pairs={{1,0},{2,1},{3,2},{0,3},{5,4},{6,5},{7,6},{4,7},{9,8},{10,9},{11,1... | collective-permute-start | bytes 110600 | tf_op jit(solution)/shard_map/ppermute | solution.py:21
  363.1 14.5 %copy-start.1 = (f32[2,64,256]{2,1,0:T(8,128)S(1)}, f32[2,64,256]{2,1,0:T(8,128)}, u32[]{:S(2)}) copy-start(f32[2,64,256]{2,1,0:T(8,128)} %param.8) | copy-start | bytes 393220
where the time goes:
time: 385 us; the launch traced here: 378 us
  blocking collectives  94.9 us (25%)
  local copies, waits for them, and re-layouts  92 us (24%)
  matrix products  65.8 us (17%)
  starting transfers between devices  57.1 us (15%)
  waiting for transfers between devices  47.6 us (12%)
  other arithmetic  19.2 us (5%)
    all_to_all x2, blocking collectives, inverse_transform(): lax.all_to_all(summed, 'slab', split_axis=2, concat_axis=3, tiled=True)  39.5 us
    all_to_all x1, blocking collectives, forward_transform(): lax.all_to_all(mixed, 'slab', split_axis=3, concat_axis=2, tiled=True)  31 us
    another operation x2, local copies, waits for them, and re-layouts  28.3 us
    reshape x1, local copies, waits for them, and re-layouts, on_device(): grad_fine = jnp.einsum('oiabc,oxyz->ixaybzc', kernel_down, grad_down, pre...  18.4 us
    unnamed x35, local copies, waits for them, and re-layouts  17.3 us
    ppermute x4, starting transfers between devices, with_halo(): lax.ppermute(lax.slice_in_dim(block, block.shape[dim] - width, None, axis...  14.9 us
    all_to_all x1, blocking collectives, forward_transform(): lax.all_to_all(spectrum, 'pencil', split_axis=3, concat_axis=4, tiled=True)  14.8 us
    all_to_all x1, starting transfers between devices, forward_transform(): lax.all_to_all(mixed, 'slab', split_axis=3, concat_axis=2, tiled=True)  13.9 us
  transfers between devices with their start and end apart: 11, of which 9 were waited for; matrix products, arithmetic and copies ran while one was open for 0% of the time, Pallas kernels for 0%

commit v1 on v0

v1 whole, which is shorter than its diff:
```python
import functools

import jax
import jax.numpy as jnp
import ml_dtypes
import numpy as np
from jax import lax
from jax.experimental import pallas as pl
from jax.experimental.pallas import tpu as pltpu
from jax.sharding import PartitionSpec as P

MESH = pl.DeviceIdType.MESH
BF = jnp.bfloat16
F32 = jnp.float32
N = 256
GROWTH = 3.0
TWO_PI = 2.0 * np.pi
KINDS = (F32, F32, F32, F32, BF, F32, F32, F32)


def theta(a, b):
    return TWO_PI * ((a[:, None].astype(np.int64) * b[None, :]) % N) / N


def grid(*sizes):
    return [g.reshape(-1) for g in np.meshgrid(*[np.arange(s) for s in sizes], indexing="ij")]


def signed(k):
    return np.where(k < N // 2, k, k - N)


def wave(k):
    return np.where(k == N // 2, 0, signed(k)) * (TWO_PI / N)


def complex_rows(angle, c_out, c_in, sign, turn):
    value = np.exp(1j * sign * angle) * (1j**turn)
    a, b = c_out[:, None], c_in[None, :]
    same = a == b
    cross = np.where((a == 0) & (b == 1), -value.imag, value.imag)
    return np.where(same, value.real, cross)


def swap_rows(order_in, order_out, sign):
    rows_in = {key: i for i, key in enumerate(order_in)}
    count = len(order_in)
    out = np.zeros((2 * count, count))
    for i, key in enumerate(order_out):
        out[i, rows_in[key]] = 1.0
        name = dict(key)
        name["c"] = 1 - name["c"]
        other = tuple(name.items())
        out[count + i, rows_in[other]] = (1.0 if dict(key)["c"] == 0 else -1.0) * (-sign)
    return out


def keys(spec, canon):
    names = [n for n, _ in spec]
    axes = grid(*[s for _, s in spec])
    out = []
    for values in zip(*axes):
        d = dict(zip(names, (int(v) for v in values)))
        out.append(tuple((n, d[n]) for n in canon))
    return out


def tables():
    t = {}
    half = np.where(np.arange(N // 2) == 0, 1.0, 2.0) / float(N) ** 3
    z = np.arange(N)
    q, c, k = grid(16, 2, 8)
    kz = 8 * q + k
    t["zf"] = complex_rows(theta(kz, z), c, np.zeros(N, np.int64), -1, 0)
    par, zz = grid(2, 128)
    zc = 2 * zz + par
    back = complex_rows(theta(kz, zc), c, np.zeros(N, np.int64), -1, 0) * half[kz][:, None]
    t["zb"] = np.stack([back, back * wave(kz)[:, None]])
    q, k, c = grid(16, 8, 2)
    kz = 8 * q + k
    inv = complex_rows(theta(kz, zc).T, np.zeros(N, np.int64), c, 1, 0).T * half[kz][:, None]
    t["zi"] = np.stack([inv, inv * wave(kz)[:, None]])
    t["zj"] = complex_rows(theta(kz, z).T, np.zeros(N, np.int64), c, 1, 0).T
    a = np.arange(N)
    base = np.concatenate([np.cos(theta(a, a)), np.sin(theta(a, a))], axis=0)
    qy = wave(a)
    t["yt"] = base
    times = np.concatenate([qy, qy])[:, None] * base
    t["yi"] = np.concatenate([times, base], axis=1)
    by = base * qy[None, :]
    t["yb"] = np.concatenate([by, base], axis=0)
    x1, c_out, kx = grid(2, 2, N)
    r, w, c_in = grid(32, 4, 2)
    pos = lambda x1: 128 * (w // 2) + 4 * r + 2 * (w % 2) + x1
    full = [complex_rows(theta(kx[:512], pos(v)), c_out[:512], c_in, -1, 0) for v in (0, 1)]
    t["xf"] = np.concatenate(full, axis=0)
    c_k, kx = grid(2, N)
    t["xj"] = np.concatenate(
        [complex_rows(theta(kx, pos(v)).T, c_in, c_k, 1, -1) for v in (0, 1)], axis=0
    )
    r, c, x8 = grid(32, 2, 8)
    t["xi"] = complex_rows(theta(kx, 8 * r + x8).T, c, c_k, 1, 1)
    r, x8, c = grid(32, 8, 2)
    t["xb"] = complex_rows(theta(kx, 8 * r + x8), c_k, c, -1, 0)
    pairs = {}
    for name, value in t.items():
        high = value.astype(np.float32).astype(ml_dtypes.bfloat16)
        low = (value - high.astype(np.float64)).astype(np.float32).astype(ml_dtypes.bfloat16)
        pairs[name] = np.stack([high, low])
    canon = ("w", "c", "k")
    s = {}
    s["pf"] = swap_rows(
        keys((("w", 4), ("c", 2), ("k", 8)), canon), keys((("k", 8), ("w", 4), ("c", 2)), canon), -1
    )
    s["pj"] = swap_rows(
        keys((("k", 8), ("w", 4), ("c", 2)), canon), keys((("w", 4), ("k", 8), ("c", 2)), canon), 1
    )
    s["pi"] = swap_rows(
        keys((("k", 8), ("c", 2), ("w", 8)), canon), keys((("w", 8), ("k", 8), ("c", 2)), canon), 1
    )
    s["pb"] = swap_rows(
        keys((("w", 8), ("c", 2), ("k", 8)), canon), keys((("k", 8), ("w", 8), ("c", 2)), canon), -1
    )
    par, i, a, y = grid(2, 3, 2, 16)
    e2 = np.zeros((192, 24))
    e2[np.arange(192), 8 * i + 4 * a + 2 * (y % 2) + par] = 1.0
    s["e2t"] = e2
    e1 = np.zeros((384, 48))
    e1[np.arange(384), np.arange(384) % 48] = 1.0
    s["e1"] = e1
    for name, value in s.items():
        pairs[name] = value.astype(np.float32).astype(ml_dtypes.bfloat16)
    return pairs


def dot(a, b, ca, cb):
    return lax.dot_general(a, b, (((ca,), (cb,)), ((), ())), preferred_element_type=F32)


def nn(a, b):
    return dot(a, b, 1, 0)


def nt(a, b):
    return dot(a, b, 1, 1)


def tn(a, b):
    return dot(a, b, 0, 0)


def roll(x, shift):
    return pltpu.roll(x, shift % x.shape[-1], x.ndim - 1)


def split(x):
    high = x.astype(BF)
    return high, (x - high.astype(F32)).astype(BF)


def lanes():
    return lax.broadcasted_iota(jnp.int32, (1, 128), 1)


def low_halves(a, b):
    return jnp.where(lanes() < 64, a, roll(b, 64))


def high_halves(a, b):
    return jnp.where(lanes() < 64, roll(a, 64), b)


def transpose_groups(tiles):
    tiles = list(tiles)
    for d in (1, 2, 4):
        odd = (lanes() // (16 * d)) % 2 == 1
        for i in range(8):
            if i & d:
                continue
            low, high = tiles[i], tiles[i + d]
            tiles[i] = jnp.where(odd, roll(high, 16 * d), low)
            tiles[i + d] = jnp.where(odd, high, roll(low, 128 - 16 * d))
    return tiles


def cat(parts, axis):
    return jnp.concatenate(list(parts), axis=axis)


def parts_of(x, kind):
    return (x.astype(BF),) if kind == BF else split(x)


def pair_swapped(moved, rows, fields):
    return [
        cat([moved[:rows, 256 * f : 256 * f + 256], moved[rows:, 256 * f : 256 * f + 256]], 1)
        for f in range(fields)
    ]


def table_left(form, t, x, index=()):
    high, low = t[(0, *index)], t[(1, *index)]
    out = form(high, x[0]) + form(low, x[0])
    if len(x) > 1:
        out = out + form(high, x[1])
    return out


def table_right(form, x, t, index=()):
    high, low = t[(0, *index)], t[(1, *index)]
    out = form(x[0], high) + form(x[0], low)
    if len(x) > 1:
        out = out + form(x[1], high)
    return out


def stage_z_forward(t, density):
    return table_left(nt, t["zf"], split(density)).reshape(16, 16, 128)


def stage_y_forward(t, got):
    z_rows = [got[4 * i : 4 * i + 4].reshape(64, 128).astype(F32) for i in range(4)]
    x = cat(
        [f(z_rows[2 * a], z_rows[2 * a + 1]) for f in (low_halves, high_halves) for a in (0, 1)], 1
    )
    left = [
        cat(pair_swapped(nn(t["pf"][...], part).astype(BF), 64, 2), 0)
        for part in parts_of(x, got.dtype)
    ]
    out = table_right(nn, left, t["yt"])
    first, second = out[:64], out[64:]
    parts = []
    for a in (0, 1):
        u, v = first[:, 128 * a : 128 * a + 128], second[:, 128 * a : 128 * a + 128]
        parts += [low_halves(u, v), high_halves(u, v)]
    return jnp.stack([p.reshape(8, 8, 128) for p in parts], axis=1).reshape(32, 8, 128)


def factors(q, r):
    kz = 8 * q + r // 4
    row = lax.broadcasted_iota(jnp.int32, (N, 128), 0)
    lane = lax.broadcasted_iota(jnp.int32, (N, 128), 1)
    ky = 64 * (r % 4) + lane % 64
    spacing = F32(TWO_PI / N)

    def full(k):
        return jnp.where(k < N // 2, k, k - N).astype(F32) * spacing

    fx, fy = full(row), full(ky)
    fz = (kz + 0 * row).astype(F32) * spacing
    square = fx * fx + fy * fy + fz * fz
    anchor = (row == 0) & (ky == 0) & (kz == 0)
    square = jnp.where(anchor, F32(1.0), square)
    qx = jnp.where(row == N // 2, F32(0.0), fx)
    first = lane < 64
    inverse = F32(GROWTH) / square
    return inverse, jnp.where(first, inverse, inverse * qx), jnp.where(first, qx, F32(1.0))


def times_rows(x, factor):
    return (x.reshape(2, N, 128) * factor[None]).reshape(2 * N, 128)


def stage_x_forward(t, got, factor):
    y = table_left(nn, t["xf"], split(got.reshape(256, 128)))
    z = jnp.where(lanes() < 64, y[:512], y[512:])
    modes = times_rows(z + roll(z, 64), factor)
    return table_left(nn, t["xi"], split(modes)).reshape(32, 16, 128)


def stage_y_inverse(t, got):
    kind = got.dtype
    got = got.reshape(8, 4, 16, 128)
    tile = [got[:, i].reshape(128, 128).astype(F32) for i in range(4)]
    x = cat([f(tile[2 * a], tile[2 * a + 1]) for f in (low_halves, high_halves) for a in (0, 1)], 1)
    left = [
        pair_swapped(nn(t["pi"][...], part).astype(BF), 128, 2) for part in parts_of(x, kind)
    ]
    ox = table_right(nn, [p[1] for p in left], t["yt"])
    oyz = table_right(nn, [p[0] for p in left], t["yi"])
    fields = (ox, oyz[:, :256], oyz[:, 256:])
    tiles = [
        cat([f[16 * i : 16 * i + 16, 128 * h : 128 * h + 128] for f in fields for h in (0, 1)], 0)
        for i in range(8)
    ]
    tiles = transpose_groups(tiles)
    return jnp.stack(
        [tiles[i].reshape(3, 2, 16, 128)[:, h] for h in (0, 1) for i in range(8)], axis=0
    )


def stage_z_inverse(t, got):
    psi = []
    for i in range(3):
        m = got[:, i].reshape(256, 128)
        psi.append(
            table_right(tn, parts_of(m, got.dtype), t["zi"], (1 if i == 2 else 0,)).astype(BF)
        )
    rows = []
    for par in (0, 1):
        for i in range(3):
            for a in (0, 1):
                rows.append(
                    cat(
                        [
                            psi[i][32 * x + 16 * a : 32 * x + 16 * a + 16, 128 * par : 128 * par + 128]
                            for x in range(4)
                        ],
                        1,
                    )
                )
    return cat(rows, 0)


def stage_z_backward(t, grad):
    out = []
    for i in range(3):
        block = []
        for x in range(4):
            for a in (0, 1):
                block.append(
                    cat(
                        [
                            grad[
                                16 * (6 * par + 2 * i + a) : 16 * (6 * par + 2 * i + a) + 16,
                                128 * x : 128 * x + 128,
                            ]
                            for par in (0, 1)
                        ],
                        1,
                    )
                )
        field = cat(block, 0)
        o = table_left(nt, t["zb"], split(field), (1 if i == 2 else 0,))
        out.append(o.reshape(16, 16, 128))
    return jnp.stack(out, axis=1)


def stage_y_backward(t, got):
    tiles = [
        cat([got[8 * h + i, f] for f in range(3) for h in (0, 1)], 0).astype(F32) for i in range(8)
    ]
    tiles = transpose_groups(tiles)
    x = cat(
        [
            cat([tiles[i][16 * (2 * f + h) : 16 * (2 * f + h) + 16] for i in range(8)], 0)
            for f in range(3)
            for h in (0, 1)
        ],
        1,
    )
    pairs = [
        pair_swapped(nn(t["pb"][...], part).astype(BF), 128, 3) for part in parts_of(x, got.dtype)
    ]
    gx = table_right(nn, [p[0] for p in pairs], t["yt"])
    rest = table_right(nn, [cat(p[1:], 1) for p in pairs], t["yb"])
    parts = []
    for a in (0, 1):
        u, v = gx[:, 128 * a : 128 * a + 128], rest[:, 128 * a : 128 * a + 128]
        parts += [low_halves(u, v), high_halves(u, v)]
    return jnp.stack([p.reshape(8, 16, 128) for p in parts], axis=1).reshape(32, 16, 128)


def stage_x_backward(t, got, inverse, along):
    y = times_rows(table_left(nn, t["xb"], parts_of(got.reshape(512, 128), got.dtype)), along)
    modes = times_rows(y + roll(y, 64), inverse)
    o = table_left(nn, t["xj"], split(modes))
    return jnp.where(lanes() < 64, o[:256], o[256:]).reshape(32, 8, 128)


def stage_y_final(t, got):
    kind = got.dtype
    got = got.reshape(8, 4, 8, 128)
    tile = [got[:, i].reshape(64, 128) for i in range(4)]
    x = cat([f(tile[2 * a], tile[2 * a + 1]) for f in (low_halves, high_halves) for a in (0, 1)], 1)
    lefts = [
        cat(pair_swapped(nn(t["pj"][...], part).astype(BF), 64, 2), 0)
        for part in parts_of(x, kind)
    ]
    out = table_right(nn, lefts, t["yt"])
    first, second = out[:64], out[64:]
    parts = []
    for a in (0, 1):
        u, v = first[:, 128 * a : 128 * a + 128], second[:, 128 * a : 128 * a + 128]
        parts += [low_halves(u, v), high_halves(u, v)]
    return cat([p.reshape(4, 16, 128) for p in parts], 0)


def stage_z_final(t, got):
    return table_right(tn, parts_of(got.reshape(256, 128), got.dtype), t["zj"])


def iota2(shape, dim):
    return lax.broadcasted_iota(jnp.int32, shape, dim)


def down_weights(t, wd):
    eight = nt(t["e1"][...], wd).astype(BF)
    row, col = iota2((384, 192), 0), iota2((384, 192), 1)
    w = jnp.where(row // 48 == (col % 16) // 2, nt(eight, t["e2t"][...]), 0.0).astype(BF)
    row, col = iota2((192, 384), 0), iota2((192, 384), 1)
    wt = jnp.where(col // 48 == (row % 16) // 2, nt(t["e2t"][...], eight), 0.0).astype(BF)
    return w, wt


def out_weights(t, wo):
    wide = wo.astype(F32)
    each = cat([jnp.broadcast_to(wide[j : j + 1], (8, 48)) for j in range(3)], 0).astype(BF)
    row, col = iota2((24, 384), 0), iota2((24, 384), 1)
    w = jnp.where(row % 8 == col // 48, nt(each, t["e1"][...]), 0.0).astype(BF)
    row, col = iota2((384, 24), 0), iota2((384, 24), 1)
    wt = jnp.where(row // 48 == col % 8, nt(t["e1"][...], each), 0.0).astype(BF)
    return w, wt


def bias_rows(t, b):
    out, left = 0.0, b
    for _ in range(3):
        part = left.astype(BF)
        out = out + nt(t["e1"][...], jnp.broadcast_to(part.astype(F32), (128, 48)).astype(BF))
        left = left - part.astype(F32)
    return out


def place(i):
    return (iota2((48, 432), 1) == 48 * i + iota2((48, 432), 0)).astype(F32).astype(BF)


def conv_weights(wc):
    out = 0.0
    for i in range(9):
        out = out + nn(cat([wc[9 * dx + i] for dx in range(3)], 0), place(i))
    return out.astype(BF)


def conv_weights_back(wc):
    rows = []
    for ex in range(3):
        out = 0.0
        for i in range(9):
            out = out + tn(wc[26 - 9 * ex - i], place(i))
        rows.append(out)
    return cat(rows, 0).astype(BF)


def add_taps(o):
    return o[:48, :512] + o[48:96, 128:640] + o[96:, 256:]


def add_own_taps(o):
    none = jnp.zeros((48, 128), F32)
    return o[48:96] + cat([none, o[:48, :384]], 1) + cat([o[96:, 128:], none], 1)


def gate(v):
    return 0.5 + 0.5 * jnp.tanh(0.5 * v)


TABLES = tables()
NAMES = tuple(TABLES)


Q_AHEAD = sorted(
    [(dz, dc) for dz in range(8) for dc in range(2) if dz or dc],
    key=lambda t: -(min(t[0], 8 - t[0]) + 0.3 * t[1]),
)
R_AHEAD = sorted(
    [(dx, dy) for dx in range(4) for dy in range(8) if dx or dy],
    key=lambda t: -(min(t[0], 4 - t[0]) + min(t[1], 8 - t[1])),
)
rem = lax.rem
div = lax.div


def kernel(*refs):
    args = refs[:8]
    count = len(NAMES)
    source = dict(zip(NAMES, refs[8 : 8 + count]))
    out = refs[8 + count]
    rest = refs[9 + count :]
    t = dict(zip(NAMES, rest[:count]))
    rest = rest[count:]
    here, rest = rest[:8], rest[8:]
    den, wd, bd, wc, bc, wo, obs, noi = here
    (s1, r1, s2, r2, s3, r3, s4, r4, s5, r5, s6, r6, s7, r7, s8, r8) = rest[:16]
    (fb, gb, sb, w1, w2, wb, wbt, wp, wpt, slope, pc, got_obs, got_noi, fac, bias) = rest[16:31]
    tsem, asem, ssem, rsem, hsem_s, hsem_r, osem_s, osem_r = rest[31:]

    s = lax.axis_index("slab")
    zh = lax.axis_index("pencil")
    core = rem(s, 2)
    r = rem(div(s, 2), 32)
    zl = div(s, 64)
    z = 2 * zh + zl
    q = 2 * z + core
    rx, ry = div(r, 8), rem(r, 8)

    def device(q, r):
        return {"slab": 64 * rem(div(q, 2), 2) + 2 * r + rem(q, 2), "pencil": div(q, 4)}

    def q_partners():
        for dz, dc in Q_AHEAD:
            z2 = rem(z + dz, 8) if dz else z
            c2 = 1 - core if dc else core
            yield (
                2 * z2 + c2,
                {"slab": 64 * rem(z2, 2) + 2 * r + c2, "pencil": div(z2, 2)},
            )

    def r_partners():
        for dx, dy in R_AHEAD:
            x2 = rem(rx + dx, 4) if dx else rx
            y2 = rem(ry + dy, 8) if dy else ry
            r2 = 8 * x2 + y2
            yield r2, {"slab": 64 * zl + 2 * r2 + core, "pencil": zh}

    for i in (0, *range(1, 8)):
        pltpu.make_async_copy(args[i], here[i], asem.at[i]).start()
    for i, name in enumerate(NAMES):
        pltpu.make_async_copy(source[name], t[name], tsem.at[i]).start()

    barrier = pltpu.get_barrier_semaphore()

    def greet(dev):
        pl.semaphore_signal(barrier, inc=1, device_id=dev, device_id_type=MESH)

    for _, dev in r_partners():
        greet(dev)
    for _, dev in q_partners():
        greet(dev)
    for dq in (1, 15):
        for dr in (1, 31):
            greet(device(rem(q + dq, 16), rem(r + dr, 32)))
    home = div(s, 4)
    slot = rem(s, 4)
    mine = home == r
    own = mine.astype(jnp.int32)
    for j in range(4):

        @pl.when(jnp.logical_not(mine & (rem(q, 4) == j)))
        def _():
            greet(device(4 * zh + j, home))

        @pl.when(jnp.logical_not(mine & (slot == j)))
        def _():
            greet({"slab": 4 * r + j, "pencil": zh})

    def ready(*names):
        for name in names:
            pltpu.make_async_copy(source[name], t[name], tsem.at[NAMES.index(name)]).wait()

    def have(*numbers):
        for i in numbers:
            pltpu.make_async_copy(args[i], here[i], asem.at[i]).wait()

    def send(phase, src, dst, me, partners):
        for d, dev in partners:
            pltpu.make_async_remote_copy(
                src_ref=src.at[d],
                dst_ref=dst.at[me],
                send_sem=ssem.at[phase],
                recv_sem=rsem.at[phase],
                device_id=dev,
                device_id_type=MESH,
            ).start()
        dst[me] = src[me]

    def send_q(phase, src, dst):
        send(phase, src, dst, q, q_partners())

    def send_r(phase, src, dst):
        send(phase, src, dst, r, r_partners())

    def arrived(phase, dst):
        part = dst.at[pl.ds(0, dst.shape[0] - 1)]
        pltpu.make_async_copy(part, part, rsem.at[phase]).wait()

    def sent(phase, src):
        part = src.at[pl.ds(0, src.shape[0] - 1)]
        pltpu.make_async_copy(part, part, ssem.at[phase]).wait()

    def halo(which, buf, action):
        cut = {0: ((128, 640), (128, 640)), 1: ((512, 640), (0, 128)), -1: ((128, 256), (640, 768))}
        line = {0: ((1, 9), (1, 9)), 1: ((8, 9), (0, 1)), -1: ((1, 2), (9, 10))}
        ways = ((1, 0), (-1, 0), (1, 1), (1, -1), (-1, 1), (-1, -1), (0, 1), (0, -1))
        for k, (dr, dq) in enumerate(ways):
            (a, b), (c, d) = cut[dr]
            (e, f), (g, h) = line[dq]
            copy = pltpu.make_async_remote_copy(
                src_ref=buf.at[pl.ds(e, f - e), :, pl.ds(a, b - a)],
                dst_ref=buf.at[pl.ds(g, h - g), :, pl.ds(c, d - c)],
                send_sem=hsem_s.at[which, k],
                recv_sem=hsem_r.at[which, k],
                device_id=device(rem(q + dq + 16, 16), rem(r + dr + 32, 32)),
                device_id_type=MESH,
            )
            action(copy)

    def shifted(buf, rows, tiles):
        lo, hi = rows
        for x in tiles:
            part = buf[lo:hi, :, 128 * x : 128 * x + 128].reshape(48 * (hi - lo), 128)
            for dz, value in enumerate((roll(part, 1), part, roll(part, 127))):
                sb[lo:hi, 48 * dz : 48 * dz + 48, 128 * x : 128 * x + 128] = value.reshape(
                    hi - lo, 48, 128
                )

    def conv(which, buf, weights):
        shifted(buf, (1, 9), range(1, 5))

        def inner(y, carry):
            o = nn(weights[...], sb[pl.ds(y, 3), :, 128:640].reshape(432, 512))
            pc[y] = add_own_taps(o)
            return carry

        lax.fori_loop(1, 7, inner, 0)
        halo(which, buf, lambda c: c.wait_recv())
        shifted(buf, (0, 10), (0, 5))
        shifted(buf, (0, 1), range(1, 5))
        shifted(buf, (9, 10), range(1, 5))

        def edges(y, carry):
            side = cat([sb[pl.ds(y, 3), :, 0:128], sb[pl.ds(y, 3), :, 640:768]], 2)
            o = nn(weights[...], side.reshape(432, 256))
            pc[y, :, 0:128] += o[:48, :128]
            pc[y, :, 384:512] += o[96:, 128:]
            return carry

        lax.fori_loop(1, 7, edges, 0)
        for y in (0, 7):
            pc[y] = add_taps(nn(weights[...], sb[y : y + 3].reshape(432, 768)))

    have(0)
    ready("zf")
    s1[...] = (stage_z_forward(t, den[...].reshape(128, 256))).astype(s1.dtype)
    have(6, 7)
    pl.semaphore_wait(barrier, 58 - 2 * own)
    send_q(0, s1, r1)

    def observed_copies(j, action):
        for src, dst, kind in (
            (obs.at[:, 0, pl.ds(8 * j, 8), :], got_obs.at[slot], 0),
            (noi.at[0, pl.ds(8 * j, 8), :], got_noi.at[slot], 1),
        ):
            action(
                pltpu.make_async_remote_copy(
                    src_ref=src,
                    dst_ref=dst,
                    send_sem=osem_s.at[kind, j],
                    recv_sem=osem_r.at[kind, slot],
                    device_id=device(4 * zh + j, home),
                    device_id_type=MESH,
                )
            )

    for j in range(4):
        this = mine & (rem(q, 4) == j)

        @pl.when(jnp.logical_not(this))
        def _():
            observed_copies(j, lambda c: c.start())

        @pl.when(this)
        def _():
            got_obs[slot] = obs[:, 0, 8 * j : 8 * j + 8, :]
            got_noi[slot] = noi[0, 8 * j : 8 * j + 8, :]

    inverse, both, along = factors(q, r)
    fac[0] = inverse
    fac[1] = both
    fac[2] = along
    ready("e1", "e2t")
    have(1, 2, 3, 4, 5)
    w, wt = down_weights(t, wd[...])
    wb[...] = w
    wbt[...] = wt
    w, wt = out_weights(t, wo[...])
    wp[...] = w
    wpt[...] = wt
    bias[0] = bias_rows(t, bd[...])
    bias[1] = bias_rows(t, bc[...])

    arrived(0, r1)
    ready("pf", "yt")
    s2[...] = (stage_y_forward(t, r1[...])).astype(s2.dtype)
    send_r(1, s2, r2)
    w1[...] = conv_weights(wc)
    arrived(1, r2)
    ready("xf", "xi")
    s3[...] = (stage_x_forward(t, r2[...], fac[1])).astype(s3.dtype)
    send_r(2, s3, r3)
    w2[...] = conv_weights_back(wc)
    arrived(2, r3)
    ready("pi", "yi")
    s4[...] = (stage_y_inverse(t, r3[...])).astype(s4.dtype)
    send_q(3, s4, r4)
    ready("zi", "zb", "pb", "yb", "xb", "xj", "pj", "zj")
    arrived(3, r4)

    cells = stage_z_inverse(t, r4[...])
    v = nn(wb[...], cells) + cat([bias[0]] * 4, 1)
    g = gate(v)
    fb[1:9, :, 128:640] = (v * g).astype(BF).reshape(8, 48, 512)
    halo(0, fb, lambda c: c.start())
    slope[...] = g * (1.0 + v * (1.0 - g))
    conv(0, fb, w1)

    for j in range(4):

        @pl.when(jnp.logical_not(mine & (slot == j)))
        def _():
            pltpu.make_async_copy(got_obs.at[j], got_obs.at[j], osem_r.at[0, j]).wait()
            pltpu.make_async_copy(got_noi.at[j], got_noi.at[j], osem_r.at[1, j]).wait()

    v = pc[...].reshape(384, 512) + cat([bias[1]] * 4, 1)
    g = gate(v)
    hidden = (v * g).astype(BF)
    predicted = nn(wp[...], hidden)
    seen = cat([got_obs[x].reshape(24, 128) for x in range(4)], 1)
    weight = cat([cat([got_noi[x]] * 3, 0) for x in range(4)], 1)
    residual = weight * (predicted - seen)
    high, low = split(residual)
    back = nn(wpt[...], high) + nn(wpt[...], low)
    grad_conv = (back * (g * (1.0 + v * (1.0 - g)))).astype(BF)
    gb[1:9, :, 128:640] = grad_conv.reshape(8, 48, 512)
    halo(1, gb, lambda c: c.start())
    conv(1, gb, w2)
    grad_down = (pc[...].reshape(384, 512) * slope[...]).astype(BF)
    s5[...] = (stage_z_backward(t, nn(wbt[...], grad_down))).astype(s5.dtype)

    send_q(4, s5, r5)
    arrived(4, r5)
    s6[...] = (stage_y_backward(t, r5[...])).astype(s6.dtype)
    send_r(5, s6, r6)
    arrived(5, r6)
    s7[...] = (stage_x_backward(t, r6[...], fac[0], fac[2])).astype(s7.dtype)
    send_r(6, s7, r7)
    arrived(6, r7)
    s8[...] = (stage_y_final(t, r7[...])).astype(s8.dtype)
    send_q(7, s8, r8)
    for phase, ref in enumerate((s1, s2, s3, s4, s5, s6, s7)):
        sent(phase, ref)
    halo(0, fb, lambda c: c.wait_send())
    halo(1, gb, lambda c: c.wait_send())
    for j in range(4):

        @pl.when(jnp.logical_not(mine & (rem(q, 4) == j)))
        def _():
            observed_copies(j, lambda c: c.wait_send())

    arrived(7, r8)
    out[...] = stage_z_final(t, r8[...]).reshape(2, 64, 256)
    sent(7, s8)


def on_device(
    density, weight_down, bias_down, weight_conv, bias_conv, weight_out, observed, noise_precision
):
    vmem = pl.BlockSpec(memory_space=pltpu.VMEM)
    shapes = [(v.shape, BF) for v in TABLES.values()]
    inputs = (
        density,
        weight_down.T,
        bias_down.reshape(1, -1),
        weight_conv,
        bias_conv.reshape(1, -1),
        weight_out,
        observed,
        noise_precision,
    )
    shapes += [(v.shape, v.dtype) for v in inputs]
    wide, one = (16, 16, 128), (32, 8, 128)
    two, three = (32, 16, 128), (16, 3, 16, 128)
    for shape, kind in zip((wide, one, two, three, three, two, one, wide), KINDS):
        shapes += [(shape, kind)] * 2
    shapes += [
        ((10, 48, 768), BF),
        ((10, 48, 768), BF),
        ((10, 144, 768), BF),
        ((144, 432), BF),
        ((144, 432), BF),
        ((384, 192), BF),
        ((192, 384), BF),
        ((24, 384), BF),
        ((384, 24), BF),
        ((384, 512), F32),
        ((8, 48, 512), F32),
        ((4, 3, 8, 128), F32),
        ((4, 8, 128), F32),
        ((3, N, 128), F32),
        ((2, 384, 128), F32),
    ]
    dma = pltpu.SemaphoreType.DMA
    return pl.pallas_call(
        kernel,
        out_shape=jax.ShapeDtypeStruct((2, 64, 256), F32),
        in_specs=[pl.BlockSpec(memory_space=pltpu.HBM)] * (8 + len(NAMES)),
        out_specs=vmem,
        scratch_shapes=[pltpu.VMEM(shape, kind) for shape, kind in shapes]
        + [
            dma((len(NAMES),)),
            dma((8,)),
            dma((8,)),
            dma((8,)),
            dma((2, 8)),
            dma((2, 8)),
            dma((2, 4)),
            dma((2, 4)),
        ],
        compiler_params=pltpu.CompilerParams(
            collective_id=0, has_side_effects=True, vmem_limit_bytes=64 * 1024 * 1024
        ),
    )(
        *inputs,
        *[jnp.asarray(TABLES[name]) for name in NAMES],
    )


def solution(mesh):
    return jax.shard_map(
        on_device,
        mesh=mesh,
        in_specs=(
            P("slab", "pencil", None),
            P(),
            P(),
            P(),
            P(),
            P(),
            P(None, "slab", "pencil", None),
            P("slab", "pencil", None),
        ),
        out_specs=P("slab", "pencil", None),
        check_vma=False,
    )
```

time: 385 us -> 101 us (0.26); the launches traced: 378 us -> 100 us
  Pallas kernels: 0 us -> 98.9 us
  blocking collectives: 94.9 us -> 0 us
  local copies, waits for them, and re-layouts: 92 us -> 1.57 us
  matrix products: 65.8 us -> 0 us
  starting transfers between devices: 57.1 us -> 0 us
  waiting for transfers between devices: 47.6 us -> 0 us
  other arithmetic: 19.2 us -> 0 us
    pallas_call x0 -> x1, Pallas kernels: none -> 98.9 us  [on_device(): pl.pallas_call(kernel, out_shape=jax.ShapeDtypeStruct((2, 64, 256), F32),...]
    all_to_all x5 -> x0, blocking collectives: 94.9 us -> none  [the longest x2 39.5 us: inverse_transform(): lax.all_to_all(summed, 'slab', split_axis=2, concat_axis=3, tiled=True)]
    dot_general x45 -> x0, matrix products: 65.8 us -> none  [the longest x17 13.4 us: stencil(): jnp.einsum('toc,tcxyz->oxyz', weights[first_tap:first_tap + 3], stacked,...]
    another operation x20 -> x0, local copies, waits for them, and re-layouts: 36.3 us -> none
    all_to_all x3 -> x0, waiting for transfers between devices: 30.9 us -> none  [the longest x1 12.1 us: inverse_transform(): lax.all_to_all(mixed, 'pencil', split_axis=4, concat_axis=3, tiled=True)]
    ppermute x8 -> x0, starting transfers between devices: 28.8 us -> none  [the longest x4 14.9 us: with_halo(): lax.ppermute(lax.slice_in_dim(block, block.shape[dim] - width, None, axis...]
    all_to_all x3 -> x0, starting transfers between devices: 28.4 us -> none  [the longest x1 13.9 us: forward_transform(): lax.all_to_all(mixed, 'slab', split_axis=3, concat_axis=2, tiled=True)]
    reshape x1 -> x0, local copies, waits for them, and re-layouts: 18.4 us -> none  [on_device(): grad_fine = jnp.einsum('oiabc,oxyz->ixaybzc', kernel_down, grad_down, pre...]
  transfers between devices with their start and end apart: 11 -> 0, of which waited for: 9 -> 0; matrix products, arithmetic and copies ran while one was open for 0% -> 0% of each run, Pallas kernels for 0% -> 0%
where the time goes in v1:
time: 101 us; the launch traced here: 100 us
  Pallas kernels  98.9 us (98%)
  local copies, waits for them, and re-layouts  1.57 us (2%)
    pallas_call x1, Pallas kernels, on_device(): pl.pallas_call(kernel, out_shape=jax.ShapeDtypeStruct((2, 64, 256), F32),...  98.9 us

profile of v1, /device:TPU:1, one launch (start us, length us, event | category | flops | bytes accessed | tf_op | source)
XLA Modules:
  0.0 100.4 jit_solution(8735682546659429090)
XLA Ops:
  0.0 98.9 %shard_map.235 = f32[2,64,256]{2,1,0:T(8,128)} custom-call(f32[2,64,256]{2,1,0:T(8,128)} %refs_0_.1, bf16[24,48]{1,0:T(8,128)(2,1)} %bitcast.3, f32[1,48]{1,0:T(1,128)} %bitcast.4, bf16[27,48,48]{2,1,0:T(8,128)(2,1)} %refs_3_.1, f32[1,48]{1,0:T(1,128)} %bitcast.5, bf16[3,48]{1,0:T(4,128)(2,1)} %refs_5_.1, f32[3,1,32,128]{3,2,1,0:T(8,128)} %refs_6_.1, ...), custom_call_target="tpu_custom_call" | custom-call | tf_op jit(solution)/shard_map/pallas_call | solution.py:794
  98.9 1.6 %copy.27 = f32[2,64,256]{2,1,0:T(8,128)} copy(f32[2,64,256]{2,1,0:T(8,128)} %shard_map.235) | data formatting | bytes 262144

commit v2 on v1

--- a/solution.py
+++ b/solution.py
@@ -89,19 +89,25 @@
     t["yi"] = np.concatenate([times, base], axis=1)
     by = base * qy[None, :]
     t["yb"] = np.concatenate([by, base], axis=0)
-    x1, c_out, kx = grid(2, 2, N)
+    par, c_k, k2 = grid(2, 2, N // 2)
+    kx = 2 * k2 + par
     r, w, c_in = grid(32, 4, 2)
     pos = lambda x1: 128 * (w // 2) + 4 * r + 2 * (w % 2) + x1
-    full = [complex_rows(theta(kx[:512], pos(v)), c_out[:512], c_in, -1, 0) for v in (0, 1)]
-    t["xf"] = np.concatenate(full, axis=0)
-    c_k, kx = grid(2, N)
+    t["xf"] = np.concatenate(
+        [complex_rows(theta(kx, pos(v)), c_k, c_in, -1, 0) for v in (0, 1)], axis=0
+    )
     t["xj"] = np.concatenate(
         [complex_rows(theta(kx, pos(v)).T, c_in, c_k, 1, -1) for v in (0, 1)], axis=0
     )
-    r, c, x8 = grid(32, 2, 8)
-    t["xi"] = complex_rows(theta(kx, 8 * r + x8).T, c, c_k, 1, 1)
-    r, x8, c = grid(32, 8, 2)
-    t["xb"] = complex_rows(theta(kx, 8 * r + x8), c_k, c, -1, 0)
+    c_h, k2 = grid(2, N // 2)
+    r, c, x8 = grid(16, 2, 8)
+    t["xi"] = np.stack(
+        [complex_rows(theta(2 * k2 + p, 8 * r + x8).T, c, c_h, 1, 1) for p in (0, 1)]
+    )
+    r, x8, c = grid(16, 8, 2)
+    t["xb"] = np.stack(
+        [complex_rows(theta(2 * k2 + p, 8 * r + x8), c_h, c, -1, 0) for p in (0, 1)]
+    )
     pairs = {}
     for name, value in t.items():
         high = value.astype(np.float32).astype(ml_dtypes.bfloat16)
@@ -243,29 +249,34 @@
     ky = 64 * (r % 4) + lane % 64
     spacing = F32(TWO_PI / N)
 
+    kx = 2 * (row % 128) + row // 128
+
     def full(k):
         return jnp.where(k < N // 2, k, k - N).astype(F32) * spacing
 
-    fx, fy = full(row), full(ky)
+    fx, fy = full(kx), full(ky)
     fz = (kz + 0 * row).astype(F32) * spacing
     square = fx * fx + fy * fy + fz * fz
-    anchor = (row == 0) & (ky == 0) & (kz == 0)
+    anchor = (kx == 0) & (ky == 0) & (kz == 0)
     square = jnp.where(anchor, F32(1.0), square)
-    qx = jnp.where(row == N // 2, F32(0.0), fx)
+    qx = jnp.where(kx == N // 2, F32(0.0), fx)
     first = lane < 64
     inverse = F32(GROWTH) / square
     return inverse, jnp.where(first, inverse, inverse * qx), jnp.where(first, qx, F32(1.0))
 
 
 def times_rows(x, factor):
-    return (x.reshape(2, N, 128) * factor[None]).reshape(2 * N, 128)
+    half = N // 2
+    return (x.reshape(2, 2, half, 128) * factor.reshape(2, 1, half, 128)).reshape(2 * N, 128)
 
 
 def stage_x_forward(t, got, factor):
     y = table_left(nn, t["xf"], split(got.reshape(256, 128)))
     z = jnp.where(lanes() < 64, y[:512], y[512:])
     modes = times_rows(z + roll(z, 64), factor)
-    return table_left(nn, t["xi"], split(modes)).reshape(32, 16, 128)
+    even = table_left(nn, t["xi"], split(modes[:256]), (0,))
+    odd = table_left(nn, t["xi"], split(modes[256:]), (1,))
+    return cat([even + odd, even - odd], 0).reshape(32, 16, 128)
 
 
 def stage_y_inverse(t, got):
@@ -362,7 +373,11 @@
 
 
 def stage_x_backward(t, got, inverse, along):
-    y = times_rows(table_left(nn, t["xb"], parts_of(got.reshape(512, 128), got.dtype)), along)
+    planes = got.reshape(512, 128).astype(F32)
+    low, high = planes[:256], planes[256:]
+    even = table_left(nn, t["xb"], split(low + high), (0,))
+    odd = table_left(nn, t["xb"], split(low - high), (1,))
+    y = times_rows(cat([even, odd], 0), along)
     modes = times_rows(y + roll(y, 64), inverse)
     o = table_left(nn, t["xj"], split(modes))
     return jnp.where(lanes() < 64, o[:256], o[256:]).reshape(32, 8, 128)
@@ -514,10 +529,16 @@
             r2 = 8 * x2 + y2
             yield r2, {"slab": 64 * zl + 2 * r2 + core, "pencil": zh}
 
-    for i in (0, *range(1, 8)):
+    first = NAMES.index("zf")
+
+    def load(i):
         pltpu.make_async_copy(args[i], here[i], asem.at[i]).start()
-    for i, name in enumerate(NAMES):
-        pltpu.make_async_copy(source[name], t[name], tsem.at[i]).start()
+
+    def load_table(i):
+        pltpu.make_async_copy(source[NAMES[i]], t[NAMES[i]], tsem.at[i]).start()
+
+    load(0)
+    load_table(first)
 
     barrier = pltpu.get_barrier_semaphore()
 
@@ -545,6 +566,12 @@
         def _():
             greet({"slab": 4 * r + j, "pencil": zh})
 
+    for i in (6, 7, *range(1, 6)):
+        load(i)
+    for i in range(len(NAMES)):
+        if i != first:
+            load_table(i)
+
     def ready(*names):
         for name in names:
             pltpu.make_async_copy(source[name], t[name], tsem.at[NAMES.index(name)]).wait()
@@ -580,15 +607,15 @@
         pltpu.make_async_copy(part, part, ssem.at[phase]).wait()
 
     def halo(which, buf, action):
-        cut = {0: ((128, 640), (128, 640)), 1: ((512, 640), (0, 128)), -1: ((128, 256), (640, 768))}
+        cut = {0: ((1, 5), (1, 5)), 1: ((4, 5), (0, 1)), -1: ((1, 2), (5, 6))}
         line = {0: ((1, 9), (1, 9)), 1: ((8, 9), (0, 1)), -1: ((1, 2), (9, 10))}
         ways = ((1, 0), (-1, 0), (1, 1), (1, -1), (-1, 1), (-1, -1), (0, 1), (0, -1))
         for k, (dr, dq) in enumerate(ways):
             (a, b), (c, d) = cut[dr]
             (e, f), (g, h) = line[dq]
             copy = pltpu.make_async_remote_copy(
-                src_ref=buf.at[pl.ds(e, f - e), :, pl.ds(a, b - a)],
-                dst_ref=buf.at[pl.ds(g, h - g), :, pl.ds(c, d - c)],
+                src_ref=buf.at[pl.ds(a, b - a), pl.ds(e, f - e)],
+                dst_ref=buf.at[pl.ds(c, d - c), pl.ds(g, h - g)],
                 send_sem=hsem_s.at[which, k],
                 recv_sem=hsem_r.at[which, k],
                 device_id=device(rem(q + dq + 16, 16), rem(r + dr + 32, 32)),
@@ -599,11 +626,15 @@
     def shifted(buf, rows, tiles):
         lo, hi = rows
         for x in tiles:
-            part = buf[lo:hi, :, 128 * x : 128 * x + 128].reshape(48 * (hi - lo), 128)
+            part = buf[x, lo:hi].reshape(48 * (hi - lo), 128)
             for dz, value in enumerate((roll(part, 1), part, roll(part, 127))):
                 sb[lo:hi, 48 * dz : 48 * dz + 48, 128 * x : 128 * x + 128] = value.reshape(
                     hi - lo, 48, 128
                 )
+
+    def fill(buf, value):
+        for x in range(4):
+            buf[x + 1, 1:9] = value[:, 128 * x : 128 * x + 128].reshape(8, 48, 128)
 
     def conv(which, buf, weights):
         shifted(buf, (1, 9), range(1, 5))
@@ -700,7 +731,7 @@
     cells = stage_z_inverse(t, r4[...])
     v = nn(wb[...], cells) + cat([bias[0]] * 4, 1)
     g = gate(v)
-    fb[1:9, :, 128:640] = (v * g).astype(BF).reshape(8, 48, 512)
+    fill(fb, (v * g).astype(BF))
     halo(0, fb, lambda c: c.start())
     slope[...] = g * (1.0 + v * (1.0 - g))
     conv(0, fb, w1)
@@ -722,7 +753,7 @@
     high, low = split(residual)
     back = nn(wpt[...], high) + nn(wpt[...], low)
     grad_conv = (back * (g * (1.0 + v * (1.0 - g)))).astype(BF)
-    gb[1:9, :, 128:640] = grad_conv.reshape(8, 48, 512)
+    fill(gb, grad_conv)
     halo(1, gb, lambda c: c.start())
     conv(1, gb, w2)
     grad_down = (pc[...].reshape(384, 512) * slope[...]).astype(BF)
@@ -774,8 +805,8 @@
     for shape, kind in zip((wide, one, two, three, three, two, one, wide), KINDS):
         shapes += [(shape, kind)] * 2
     shapes += [
-        ((10, 48, 768), BF),
-        ((10, 48, 768), BF),
+        ((6, 10, 48, 128), BF),
+        ((6, 10, 48, 128), BF),
         ((10, 144, 768), BF),
         ((144, 432), BF),
         ((144, 432), BF),

time: 101 us -> 99.3 us (0.983)
  Pallas kernels: 98.9 us -> 97.6 us
    pallas_call x1, Pallas kernels: 98.9 us -> 97.6 us  [on_device(): pl.pallas_call(kernel, out_shape=jax.ShapeDtypeStruct((2, 64, 256), F32),...]
where the time goes in v2:
time: 99.3 us; the launch traced here: 99.2 us
  Pallas kernels  97.6 us (98%)
  local copies, waits for them, and re-layouts  1.57 us (2%)
    pallas_call x1, Pallas kernels, on_device(): pl.pallas_call(kernel, out_shape=jax.ShapeDtypeStruct((2, 64, 256), F32),...  97.6 us

profile of v2, /device:TPU:1, one launch (start us, length us, event | category | flops | bytes accessed | tf_op | source)
XLA Modules:
  0.0 99.2 jit_solution(1208912097644097153)
XLA Ops:
  0.0 97.6 %shard_map.235 = f32[2,64,256]{2,1,0:T(8,128)} custom-call(f32[2,64,256]{2,1,0:T(8,128)} %refs_0_.1, bf16[24,48]{1,0:T(8,128)(2,1)} %bitcast.3, f32[1,48]{1,0:T(1,128)} %bitcast.4, bf16[27,48,48]{2,1,0:T(8,128)(2,1)} %refs_3_.1, f32[1,48]{1,0:T(1,128)} %bitcast.5, bf16[3,48]{1,0:T(4,128)(2,1)} %refs_5_.1, f32[3,1,32,128]{3,2,1,0:T(8,128)} %refs_6_.1, ...), custom_call_target="tpu_custom_call" | custom-call | tf_op jit(solution)/shard_map/pallas_call | solution.py:825
  97.6 1.6 %copy.27 = f32[2,64,256]{2,1,0:T(8,128)} copy(f32[2,64,256]{2,1,0:T(8,128)} %shard_map.235) | data formatting | bytes 262144

commit v3 on v2

--- a/solution.py
+++ b/solution.py
@@ -86,7 +86,7 @@
     qy = wave(a)
     t["yt"] = base
     times = np.concatenate([qy, qy])[:, None] * base
-    t["yi"] = np.concatenate([times, base], axis=1)
+    t["yi"] = times
     by = base * qy[None, :]
     t["yb"] = np.concatenate([by, base], axis=0)
     par, c_k, k2 = grid(2, 2, N // 2)
@@ -284,29 +284,26 @@
     got = got.reshape(8, 4, 16, 128)
     tile = [got[:, i].reshape(128, 128).astype(F32) for i in range(4)]
     x = cat([f(tile[2 * a], tile[2 * a + 1]) for f in (low_halves, high_halves) for a in (0, 1)], 1)
-    left = [
-        pair_swapped(nn(t["pi"][...], part).astype(BF), 128, 2) for part in parts_of(x, kind)
-    ]
-    ox = table_right(nn, [p[1] for p in left], t["yt"])
-    oyz = table_right(nn, [p[0] for p in left], t["yi"])
-    fields = (ox, oyz[:, :256], oyz[:, 256:])
-    tiles = [
-        cat([f[16 * i : 16 * i + 16, 128 * h : 128 * h + 128] for f in fields for h in (0, 1)], 0)
-        for i in range(8)
-    ]
-    tiles = transpose_groups(tiles)
-    return jnp.stack(
-        [tiles[i].reshape(3, 2, 16, 128)[:, h] for h in (0, 1) for i in range(8)], axis=0
-    )
-
-
-def stage_z_inverse(t, got):
-    psi = []
-    for i in range(3):
-        m = got[:, i].reshape(256, 128)
-        psi.append(
-            table_right(tn, parts_of(m, got.dtype), t["zi"], (1 if i == 2 else 0,)).astype(BF)
-        )
+    return [pair_swapped(nn(t["pi"][...], part).astype(BF), 128, 2) for part in parts_of(x, kind)]
+
+
+def y_inverse_field(t, left, i):
+    field = table_right(
+        nn, [p[1 if i == 0 else 0] for p in left], t["yi" if i == 1 else "yt"]
+    )
+    tiles = transpose_groups(
+        cat([field[16 * k : 16 * k + 16, 128 * h : 128 * h + 128] for h in (0, 1)], 0)
+        for k in range(8)
+    )
+    return jnp.stack([tiles[k][16 * h : 16 * h + 16] for h in (0, 1) for k in range(8)], axis=0)
+
+
+def z_inverse_field(t, got, i):
+    m = parts_of(got.reshape(256, 128), got.dtype)
+    return table_right(tn, m, t["zi"], (1 if i == 2 else 0,)).astype(BF)
+
+
+def block_cells(psi):
     rows = []
     for par in (0, 1):
         for i in range(3):
@@ -723,12 +720,17 @@
     w2[...] = conv_weights_back(wc)
     arrived(2, r3)
     ready("pi", "yi")
-    s4[...] = (stage_y_inverse(t, r3[...])).astype(s4.dtype)
-    send_q(3, s4, r4)
+    left = stage_y_inverse(t, r3[...])
+    for i in range(3):
+        s4[i] = y_inverse_field(t, left, i).astype(s4.dtype)
+        send_q((3, 8, 9)[i], s4.at[i], r4.at[i])
     ready("zi", "zb", "pb", "yb", "xb", "xj", "pj", "zj")
-    arrived(3, r4)
-
-    cells = stage_z_inverse(t, r4[...])
+
+    psi = []
+    for i in range(3):
+        arrived((3, 8, 9)[i], r4.at[i])
+        psi.append(z_inverse_field(t, r4[i], i))
+    cells = block_cells(psi)
     v = nn(wb[...], cells) + cat([bias[0]] * 4, 1)
     g = gate(v)
     fill(fb, (v * g).astype(BF))
@@ -769,8 +771,10 @@
     arrived(6, r7)
     s8[...] = (stage_y_final(t, r7[...])).astype(s8.dtype)
     send_q(7, s8, r8)
-    for phase, ref in enumerate((s1, s2, s3, s4, s5, s6, s7)):
+    for phase, ref in zip((0, 1, 2, 4, 5, 6), (s1, s2, s3, s5, s6, s7)):
         sent(phase, ref)
+    for i in range(3):
+        sent((3, 8, 9)[i], s4.at[i])
     halo(0, fb, lambda c: c.wait_send())
     halo(1, gb, lambda c: c.wait_send())
     for j in range(4):
@@ -801,8 +805,8 @@
     )
     shapes += [(v.shape, v.dtype) for v in inputs]
     wide, one = (16, 16, 128), (32, 8, 128)
-    two, three = (32, 16, 128), (16, 3, 16, 128)
-    for shape, kind in zip((wide, one, two, three, three, two, one, wide), KINDS):
+    two, three, apart = (32, 16, 128), (16, 3, 16, 128), (3, 16, 16, 128)
+    for shape, kind in zip((wide, one, two, apart, three, two, one, wide), KINDS):
         shapes += [(shape, kind)] * 2
     shapes += [
         ((6, 10, 48, 128), BF),
@@ -831,19 +835,19 @@
         + [
             dma((len(NAMES),)),
             dma((8,)),
-            dma((8,)),
-            dma((8,)),
+            dma((10,)),
+            dma((10,)),
             dma((2, 8)),
             dma((2, 8)),
             dma((2, 4)),
             dma((2, 4)),
         ],
         compiler_params=pltpu.CompilerParams(
-            collective_id=0, has_side_effects=True, vmem_limit_bytes=64 * 1024 * 1024
+            collective_id=0, has_side_effects=True, vmem_limit_bytes=50 * 1024 * 1024
         ),
     )(
-        *inputs,
-        *[jnp.asarray(TABLES[name]) for name in NAMES],
+        *[pltpu.with_memory_space_constraint(v, pltpu.HBM) for v in inputs],
+        *[pltpu.with_memory_space_constraint(jnp.asarray(TABLES[name]), pltpu.HBM) for name in NAMES],
     )
 
 

time: 99.3 us -> 97.9 us (0.986)
  no operation moved by 1% of the time
where the time goes in v3:
time: 97.9 us; the launch traced here: 97.8 us
  Pallas kernels  97.1 us (99%)
    pallas_call x1, Pallas kernels, on_device(): pl.pallas_call(kernel, out_shape=jax.ShapeDtypeStruct((2, 64, 256), F32),...  97.1 us

profile of v3, /device:TPU:1, one launch (start us, length us, event | category | flops | bytes accessed | tf_op | source)
XLA Modules:
  0.0 97.8 jit_solution(6118481958370546568)
XLA Ops:
  0.0 97.1 %shard_map.235 = f32[2,64,256]{2,1,0:T(8,128)S(1)} custom-call(f32[2,64,256]{2,1,0:T(8,128)} %refs_0_.1, bf16[24,48]{1,0:T(8,128)(2,1)} %bitcast.3, f32[1,48]{1,0:T(1,128)} %bitcast.4, bf16[27,48,48]{2,1,0:T(8,128)(2,1)} %refs_3_.1, f32[1,48]{1,0:T(1,128)} %bitcast.5, bf16[3,48]{1,0:T(4,128)(2,1)} %refs_5_.1, f32[3,1,32,128]{3,2,1,0:T(8,128)} %refs_6_.1, ...), custom_call_target="tpu_custom_call" | custom-call | tf_op jit(solution)/shard_map/pallas_call | solution.py:829
  97.1 0.7 copy.27

commit v4 on v3

--- a/solution.py
+++ b/solution.py
@@ -641,7 +641,7 @@
             pc[y] = add_own_taps(o)
             return carry
 
-        lax.fori_loop(1, 7, inner, 0)
+        lax.fori_loop(1, 7, inner, 0, unroll=2)
         halo(which, buf, lambda c: c.wait_recv())
         shifted(buf, (0, 10), (0, 5))
         shifted(buf, (0, 1), range(1, 5))
@@ -654,7 +654,7 @@
             pc[y, :, 384:512] += o[96:, 128:]
             return carry
 
-        lax.fori_loop(1, 7, edges, 0)
+        lax.fori_loop(1, 7, edges, 0, unroll=True)
         for y in (0, 7):
             pc[y] = add_taps(nn(weights[...], sb[y : y + 3].reshape(432, 768)))
 

time: 97.9 us -> 95.6 us (0.977)
  Pallas kernels: 97.1 us -> 94.9 us
    pallas_call x1, Pallas kernels: 97.1 us -> 94.9 us  [on_device(): pl.pallas_call(kernel, out_shape=jax.ShapeDtypeStruct((2, 64, 256), F32),...]
where the time goes in v4:
time: 95.6 us; the launch traced here: 95.5 us
  Pallas kernels  94.9 us (99%)
    pallas_call x1, Pallas kernels, on_device(): pl.pallas_call(kernel, out_shape=jax.ShapeDtypeStruct((2, 64, 256), F32),...  94.9 us

profile of v4, /device:TPU:1, one launch (start us, length us, event | category | flops | bytes accessed | tf_op | source)
XLA Modules:
  0.0 95.5 jit_solution(10606189245682146170)
XLA Ops:
  0.0 94.9 %shard_map.235 = f32[2,64,256]{2,1,0:T(8,128)S(1)} custom-call(f32[2,64,256]{2,1,0:T(8,128)} %refs_0_.1, bf16[24,48]{1,0:T(8,128)(2,1)} %bitcast.3, f32[1,48]{1,0:T(1,128)} %bitcast.4, bf16[27,48,48]{2,1,0:T(8,128)(2,1)} %refs_3_.1, f32[1,48]{1,0:T(1,128)} %bitcast.5, bf16[3,48]{1,0:T(4,128)(2,1)} %refs_5_.1, f32[3,1,32,128]{3,2,1,0:T(8,128)} %refs_6_.1, ...), custom_call_target="tpu_custom_call" | custom-call | tf_op jit(solution)/shard_map/pallas_call | solution.py:829
  94.9 0.7 copy.27

commit v5 on v4

--- a/solution.py
+++ b/solution.py
@@ -641,7 +641,7 @@
             pc[y] = add_own_taps(o)
             return carry
 
-        lax.fori_loop(1, 7, inner, 0, unroll=2)
+        lax.fori_loop(1, 7, inner, 0, unroll=True)
         halo(which, buf, lambda c: c.wait_recv())
         shifted(buf, (0, 10), (0, 5))
         shifted(buf, (0, 1), range(1, 5))

time: 95.6 us -> 95.6 us (level)
  no operation moved by 1% of the time
where the time goes in v5:
time: 95.6 us; the launch traced here: 95.5 us
  Pallas kernels  94.8 us (99%)
    pallas_call x1, Pallas kernels, on_device(): pl.pallas_call(kernel, out_shape=jax.ShapeDtypeStruct((2, 64, 256), F32),...  94.8 us

profile of v5, /device:TPU:1, one launch (start us, length us, event | category | flops | bytes accessed | tf_op | source)
XLA Modules:
  0.0 95.5 jit_solution(5287351172368903100)
XLA Ops:
  0.0 94.8 %shard_map.235 = f32[2,64,256]{2,1,0:T(8,128)S(1)} custom-call(f32[2,64,256]{2,1,0:T(8,128)} %refs_0_.1, bf16[24,48]{1,0:T(8,128)(2,1)} %bitcast.3, f32[1,48]{1,0:T(1,128)} %bitcast.4, bf16[27,48,48]{2,1,0:T(8,128)(2,1)} %refs_3_.1, f32[1,48]{1,0:T(1,128)} %bitcast.5, bf16[3,48]{1,0:T(4,128)(2,1)} %refs_5_.1, f32[3,1,32,128]{3,2,1,0:T(8,128)} %refs_6_.1, ...), custom_call_target="tpu_custom_call" | custom-call | tf_op jit(solution)/shard_map/pallas_call | solution.py:829
  94.8 0.7 copy.27
